TPU v7x, 128 devices: a whole 4x4x4 slice. The times are simulated.
128 devices in a mesh: pipe: 2 (over x_hi), ctx: 8 (over x_lo, z), tp: 8 (over y, core).
Axes of the slice: x: 4 (x_hi: 2, x_lo: 2; x = x_hi * 2 + x_lo), y: 4, z: 4, core: 2. Of those that a mesh axis runs over, the one named last changes fastest.
Arguments:
- queries: bfloat16 [2, 2, 4096, 8192], P('pipe', None, 'ctx', 'tp'), may hold values from -220 to 220
- keys: bfloat16 [2, 2, 4096, 1024], P('pipe', None, 'ctx', 'tp'), may hold values from -8 to 8
- values: bfloat16 [2, 2, 4096, 1024], P('pipe', None, 'ctx', 'tp'), may hold values from -16 to 16
- doc_start: int32 [2, 4096], P(None, 'ctx'), may hold values from 0 to 4095, as said below
- owners: int32 [2, 128], P(None, 'ctx'), may hold values from 0 to 7, as said below
Outputs:
- balanced: bfloat16 [2, 2, 8, 8, 3, 32, 8192], P('pipe', None, 'ctx', None, None, None, 'tp')
Inputs may be any that keep to these rules, and one draw needn't show every extreme that they name: doc_start[m, i] is the first token of token i's document: it never decreases along the slab, is at most i, i - doc_start[m, i] < 256, and every slab holds a document of exactly 256 tokens. `owners`: of the 16 tracts that lie on one index of ctx, at most 3 have the same owner, and in every such block some owner gets exactly 3.
All inputs are finite; a program needn't handle non-finite values.
Results may differ from a plain program's by a relative error of at most 0.0063.
Values may be sent and summed in bfloat16 or wider, within the bound.
A program may use at most 128 MiB of HBM per device.

v0:
```python
import math
import jax
import jax.numpy as jnp
from jax import lax
from jax.sharding import PartitionSpec as P

HEAD_WIDTH = 128
TRACTS_DEV = 16
DOCMAX = 256


def shifted(block, axis, distance):
    devices = range(lax.axis_size(axis))
    route = [(i - distance, i) for i in devices if i - distance in devices]
    return lax.ppermute(block, axis, route)


def rank_table(owner_list, owner_count, slot_count):
    tract_count = owner_list.shape[0]
    positions = jnp.arange(tract_count, dtype=jnp.int32)
    earlier = positions[None, :] < positions[:, None]
    same_owner = owner_list[:, None] == owner_list[None, :]
    rank_of = jnp.sum(same_owner & earlier, axis=1)
    owner_ids = jnp.arange(owner_count, dtype=jnp.int32)
    slot_ids = jnp.arange(slot_count, dtype=jnp.int32)
    return (owner_list[None, None, :] == owner_ids[:, None, None]) & (
        rank_of[None, None, :] == slot_ids[None, :, None]
    )


def attend_rows(query_rows, key_win, value_win, first_key, row_ids, row_starts):
    query_count = query_rows.shape[0]
    key_span = key_win.shape[0]
    kv_heads = key_win.shape[1] // HEAD_WIDTH
    query_group_width = query_rows.shape[1] // (kv_heads * HEAD_WIDTH)
    heads_for_query = query_rows.reshape(query_count, kv_heads, query_group_width, HEAD_WIDTH)
    heads_for_key = key_win.reshape(key_span, kv_heads, HEAD_WIDTH)
    value_heads = value_win.reshape(key_span, kv_heads, HEAD_WIDTH)
    scores = jnp.einsum(
        "tkgd,jkd->tkgj", heads_for_query, heads_for_key, preferred_element_type=jnp.float32
    ) / math.sqrt(HEAD_WIDTH)
    key_ids = first_key + jnp.arange(key_span, dtype=jnp.int32)
    allowed = (key_ids[None, :] >= row_starts[:, None]) & (key_ids[None, :] <= row_ids[:, None])
    scores = jnp.where(allowed[:, None, None, :], scores, -1e30)
    row_max = jnp.max(scores, axis=-1, keepdims=True)
    exp_terms = jnp.exp(scores - row_max)
    denom_sum = jnp.sum(exp_terms, axis=-1)
    weights = exp_terms.astype(jnp.bfloat16)
    attended = (
        jnp.einsum("tkgj,jkd->tkgd", weights, value_heads, preferred_element_type=jnp.float32)
        / denom_sum[..., None]
    )
    return attended.reshape(query_count, -1).astype(jnp.bfloat16)


def local(queries, keys, values, doc_start, owners):
    section_index = lax.axis_index("pipe")
    my_ctx = lax.axis_index("ctx")
    ctx_count = lax.axis_size("ctx")
    micro_count = queries.shape[1]
    rows_dev = queries.shape[2]
    width_q = queries.shape[3]
    width_kv = keys.shape[3]
    tract_rows = rows_dev // TRACTS_DEV
    slot_count = TRACTS_DEV // ctx_count + 1
    local_ids = jnp.arange(tract_rows, dtype=jnp.int32)
    carried = jnp.zeros((ctx_count, slot_count, tract_rows, width_q), jnp.bfloat16)
    tick_outputs = []
    for clock_tick in range(micro_count + 1):
        mb_index = clock_tick - section_index
        mb_pick = jnp.clip(mb_index, 0, micro_count - 1)
        own_queries = lax.dynamic_index_in_dim(queries[0], mb_pick, 0, keepdims=False)
        key_rows = lax.dynamic_index_in_dim(keys[0], mb_pick, 0, keepdims=False)
        value_rows = lax.dynamic_index_in_dim(values[0], mb_pick, 0, keepdims=False)
        own_list = lax.dynamic_index_in_dim(owners, mb_pick, 0, keepdims=False)
        send_map = rank_table(own_list, ctx_count, slot_count).astype(jnp.bfloat16)
        tract_block = own_queries.reshape(TRACTS_DEV, tract_rows, width_q)
        outgoing = jnp.einsum(
            "osk,ktf->ostf", send_map, tract_block, preferred_element_type=jnp.float32
        ).astype(jnp.bfloat16)
        arrived = lax.all_to_all(outgoing, "ctx", split_axis=0, concat_axis=0, tiled=True)
        all_keys, all_values, all_owners, all_starts = (
            lax.all_gather(key_rows, "ctx", axis=0, tiled=True),
            lax.all_gather(value_rows, "ctx", axis=0, tiled=True),
            lax.all_gather(owners, "ctx", axis=1, tiled=True),
            lax.all_gather(doc_start, "ctx", axis=1, tiled=True),
        )
        section_in = (arrived.astype(jnp.float32) + carried.astype(jnp.float32)).astype(
            jnp.bfloat16
        )
        lists = lax.dynamic_index_in_dim(all_owners, mb_pick, 0, keepdims=False).reshape(
            ctx_count, TRACTS_DEV
        )
        starts_all = lax.dynamic_index_in_dim(all_starts, mb_pick, 0, keepdims=False)

        def table_of(block_list):
            return rank_table(block_list, ctx_count, slot_count)

        tables = jax.vmap(table_of)(lists)
        mine = lax.dynamic_index_in_dim(tables, my_ctx, 1, keepdims=False)
        present = jnp.any(mine, axis=2)
        tract_pos = jnp.sum(
            mine.astype(jnp.int32) * jnp.arange(TRACTS_DEV, dtype=jnp.int32), axis=2
        )
        first_rows = (
            jnp.arange(ctx_count, dtype=jnp.int32)[:, None] * rows_dev + tract_pos * tract_rows
        )
        row_grid = first_rows[..., None] + local_ids
        start_grid = starts_all[row_grid]
        padded_keys = jnp.concatenate(
            [jnp.zeros((DOCMAX, width_kv), jnp.bfloat16), all_keys], axis=0
        )
        padded_values = jnp.concatenate(
            [jnp.zeros((DOCMAX, width_kv), jnp.bfloat16), all_values], axis=0
        )
        source_answers = []
        for source_id in range(ctx_count):
            key_win = padded_keys[source_id * rows_dev : source_id * rows_dev + rows_dev + DOCMAX]
            value_win = padded_values[
                source_id * rows_dev : source_id * rows_dev + rows_dev + DOCMAX
            ]
            slot_queries = section_in[source_id].reshape(slot_count * tract_rows, width_q)
            slot_ids = row_grid[source_id].reshape(-1)
            slot_starts = start_grid[source_id].reshape(-1)
            answer = attend_rows(
                slot_queries,
                key_win,
                value_win,
                source_id * rows_dev - DOCMAX,
                slot_ids,
                slot_starts,
            )
            source_answers.append(answer.reshape(slot_count, tract_rows, width_q))
        answers = jnp.stack(source_answers)
        owner_rows = jnp.where(present[:, :, None, None], answers, jnp.zeros_like(answers))
        if clock_tick < micro_count:
            carried = shifted(owner_rows, "pipe", 1)
        tick_outputs.append(owner_rows)
    first_section = section_index == 0
    result = jnp.stack(
        [
            jnp.where(first_section, tick_outputs[micro_id], tick_outputs[micro_id + 1])
            for micro_id in range(micro_count)
        ]
    )
    return result[None, :, None]


def solution(mesh):
    return jax.shard_map(
        local,
        mesh=mesh,
        in_specs=(
            P("pipe", None, "ctx", "tp"),
            P("pipe", None, "ctx", "tp"),
            P("pipe", None, "ctx", "tp"),
            P(None, "ctx"),
            P(None, "ctx"),
        ),
        out_specs=P("pipe", None, "ctx", None, None, None, "tp"),
        check_vma=False,
    )
```

profile of v0, /device:TPU:6, one launch (start us, length us, event | category | flops | bytes accessed | tf_op | source)
XLA Modules:
  0.0 336.8 jit_solution(15088686143844010737)
XLA Ops:
  6.5 1.9 constant_dynamic-slice_fusion.16
  8.6 1.8 constant_dynamic-slice_fusion.4
  12.7 1.7 constant_dynamic-slice_fusion
  15.3 2.0 copy.204
  17.3 6.9 %all-to-all-start = ((bf16[8,3,32,1024]{3,2,1,0:T(8,128)(2,1)}), bf16[8,3,32,1024]{3,2,1,0:T(8,128)(2,1)S(1)}, u32[]{:S(2)}, u32[]{:S(2)}) async-start(bf16[8,3,32,1024]{3,2,1,0:T(8,128)(2,1)} %copy.204), calls=%async_computation | async-start | bytes 3145728 | tf_op jit(solution)/shard_map/all_to_all | solution.py:81
  24.8 36.3 %all-gather.6 = s32[8,16,2]{1,2,0:T(2,128)S(1)} all-gather(s32[1,16,2]{1,2,0:T(2,128)S(1)} %bitcast.1570), channel_id=1, replica_groups=mesh['pipe'=2,'ctx'=8,'tp'=8] {'ctx'}, dimensions={0}, use_global_device_ids=true | all-gather | bytes 1152 | tf_op jit(solution)/shard_map/all_gather | solution.py:85
  63.8 28.1 %all_gather.30 = s32[2,4096]{1,0:T(2,128)S(1)} all-gather(s32[2,512]{1,0:T(2,128)S(1)} %copy-done.96), channel_id=1, replica_groups=mesh['pipe'=2,'ctx'=8,'tp'=8] {'ctx'}, dimensions={1}, use_global_device_ids=true | all-gather | bytes 36864 | tf_op jit(solution)/shard_map/all_gather | solution.py:86
  91.9 4.5 %gather_fusion.1 = s32[768]{0:T(1024)S(1)} fusion(s32[4096]{0:T(1024)S(1)} %bitcast.1515, s32[1024]{0:T(1024)S(1)} %pad_clamp_fusion.1), kind=kCustom, calls=%fused_computation.1 | custom fusion | bytes 9216 | tf_op jit(solution)/shard_map/gather | solution.py:109
  96.5 4.5 %gather_fusion = s32[768]{0:T(1024)S(1)} fusion(s32[4096]{0:T(1024)S(1)} %bitcast.1514, s32[1024]{0:T(1024)S(1)} %pad_clamp_fusion.2), kind=kCustom, calls=%fused_computation | custom fusion | bytes 9216 | tf_op jit(solution)/shard_map/gather | solution.py:109
  101.4 4.9 %gather_fusion.2 = s32[768]{0:T(1024)S(1)} fusion(s32[4096]{0:T(1024)S(1)} %bitcast.1513, s32[1024]{0:T(1024)S(1)} %pad_clamp_fusion), kind=kCustom, calls=%fused_computation.2 | custom fusion | bytes 9216 | tf_op jit(solution)/shard_map/gather | solution.py:109
  125.8 1.8 fusion.429
  155.9 2.0 copy.225
  158.0 3.7 %all-to-all-start.1 = ((bf16[8,3,32,1024]{3,2,1,0:T(8,128)(2,1)}), bf16[8,3,32,1024]{3,2,1,0:T(8,128)(2,1)S(1)}, u32[]{:S(2)}, u32[]{:S(2)}) async-start(bf16[8,3,32,1024]{3,2,1,0:T(8,128)(2,1)} %copy.225), calls=%async_computation.1 | async-start | bytes 3145728 | tf_op jit(solution)/shard_map/all_to_all | solution.py:81
  164.0 2.0 copy.255
  169.2 9.8 %all-to-all-done.1 = bf16[8,3,32,1024]{3,2,1,0:T(8,128)(2,1)S(1)} async-done(((bf16[8,3,32,1024]{3,2,1,0:T(8,128)(2,1)}), bf16[8,3,32,1024]{3,2,1,0:T(8,128)(2,1)S(1)}, u32[]{:S(2)}, u32[]{:S(2)}) %all-to-all-start.1) | async-done | bytes 1572896 | tf_op jit(solution)/shard_map/all_to_all | solution.py:81
  179.0 5.9 %all-to-all-start.2 = ((bf16[8,3,32,1024]{3,2,1,0:T(8,128)(2,1)}), bf16[8,3,32,1024]{3,2,1,0:T(8,128)(2,1)}, u32[]{:S(2)}, u32[]{:S(2)}) async-start(bf16[8,3,32,1024]{3,2,1,0:T(8,128)(2,1)} %copy.255), calls=%async_computation.2 | async-start | bytes 3145728 | tf_op jit(solution)/shard_map/all_to_all | solution.py:81
  184.9 15.6 %collective-permute-done = bf16[8,3,32,1024]{3,2,1,0:T(8,128)(2,1)} collective-permute-done((bf16[8,3,32,1024]{3,2,1,0:T(8,128)(2,1)}, bf16[8,3,32,1024]{3,2,1,0:T(8,128)(2,1)}, u32[]{:S(2)}, u32[]{:S(2)}) %collective-permute-start) | collective-permute-done | bytes 1572896 | tf_op jit(solution)/shard_map/ppermute | solution.py:15
  200.5 2.1 add_convert_fusion.1
  207.3 1.7 fusion.402
  214.6 1.7 fusion.399
  217.9 1.7 fusion.396
  226.0 1.7 fusion.390
  229.9 1.7 fusion.387
  233.9 1.7 fusion.384
  250.6 45.0 %collective-permute-done.1 = bf16[8,3,32,1024]{3,2,1,0:T(8,128)(2,1)} collective-permute-done((bf16[8,3,32,1024]{3,2,1,0:T(8,128)(2,1)}, bf16[8,3,32,1024]{3,2,1,0:T(8,128)(2,1)}, u32[]{:S(2)}, u32[]{:S(2)}) %collective-permute-start.1) | collective-permute-done | bytes 1572896 | tf_op jit(solution)/shard_map/ppermute | solution.py:15
  295.6 2.6 add_convert_fusion
  302.8 1.7 fusion.360
  314.2 1.7 fusion.372
  317.5 1.7 fusion.375
  320.8 1.7 fusion.378
  325.5 2.3 select_select_fusion.1
  327.8 1.9 maximum_bitcast_fusion
  (523 shorter events, 116.2 us)
Async XLA Ops:
  6.5 6.1 %copy-start.3 = (bf16[1,2,512,1024]{3,2,1,0:T(8,128)(2,1)S(1)}, bf16[1,2,512,1024]{3,2,1,0:T(8,128)(2,1)}, u32[]{:S(2)}) copy-start(bf16[1,2,512,1024]{3,2,1,0:T(8,128)(2,1)} %param.5) | copy-start | bytes 6291460
  6.5 116.6 %all-gather.16.cloned.1.call-start = ((), (), s32[]{:S(2)}) async-start(), calls=%async_computation.4 | async-start | bytes 1179648 | tf_op jit(solution)/shard_map/all_gather | solution.py:83
  8.5 117.3 %all-gather.14.cloned.1.call-start = ((), (), s32[]{:S(2)}) async-start(), calls=%async_computation.3 | async-start | bytes 1179648 | tf_op jit(solution)/shard_map/all_gather | solution.py:84
  10.4 193.5 %all-gather.20.cloned.1.call-start = ((), (), s32[]{:S(2)}) async-start(), calls=%async_computation.6 | async-start | bytes 1179648 | tf_op jit(solution)/shard_map/all_gather | solution.py:83
  11.1 196.2 %all-gather.18.cloned.1.call-start = ((), (), s32[]{:S(2)}) async-start(), calls=%async_computation.5 | async-start | bytes 1179648 | tf_op jit(solution)/shard_map/all_gather | solution.py:84
  17.3 7.5 %copy-start.89 = (s32[2,16]{1,0:T(2,128)S(1)}, s32[2,16]{1,0:T(2,128)}, u32[]{:S(2)}) copy-start(s32[2,16]{1,0:T(2,128)} %param.9) | copy-start | bytes 388
  17.3 46.5 %copy-start.96 = (s32[2,512]{1,0:T(2,128)S(1)}, s32[2,512]{1,0:T(2,128)}, u32[]{:S(2)}) copy-start(s32[2,512]{1,0:T(2,128)} %param.8) | copy-start | bytes 12292
  17.3 100.6 %all-to-all-start = ((bf16[8,3,32,1024]{3,2,1,0:T(8,128)(2,1)}), bf16[8,3,32,1024]{3,2,1,0:T(8,128)(2,1)S(1)}, u32[]{:S(2)}, u32[]{:S(2)}) async-start(bf16[8,3,32,1024]{3,2,1,0:T(8,128)(2,1)} %copy.204), calls=%async_computation | async-start | bytes 3145728 | tf_op jit(solution)/shard_map/all_to_all | solution.py:81
  24.2 275.2 %all-gather.24.cloned.1.call-start = ((), (), s32[]{:S(2)}) async-start(), calls=%async_computation.8 | async-start | bytes 1179648 | tf_op jit(solution)/shard_map/all_gather | solution.py:83
  118.1 5.0 %copy-start.77 = (pred[96,768]{1,0:T(8,128)(4,1)S(1)}, pred[96,768]{1,0:T(8,128)(4,1)}, u32[]{:S(2)}) copy-start(pred[96,768]{1,0:T(8,128)(4,1)} %get-tuple-element.103) | copy-start | bytes 221188
  144.9 5.6 %copy-start.6 = (bf16[96,1,8,128]{3,2,0,1:T(8,128)(2,1)}, bf16[96,1,8,128]{3,2,0,1:T(8,128)(2,1)S(1)}, u32[]{:S(2)}) copy-start(bf16[96,1,8,128]{3,2,0,1:T(8,128)(2,1)S(1)} %copy.212) | copy-start | bytes 589828
  145.0 7.3 %copy-start.8 = (bf16[96,1,8,128]{3,2,0,1:T(8,128)(2,1)}, bf16[96,1,8,128]{3,2,0,1:T(8,128)(2,1)S(1)}, u32[]{:S(2)}) copy-start(bf16[96,1,8,128]{3,2,0,1:T(8,128)(2,1)S(1)} %copy.214) | copy-start | bytes 589828
  145.9 7.8 %copy-start.10 = (bf16[96,1,8,128]{3,2,0,1:T(8,128)(2,1)}, bf16[96,1,8,128]{3,2,0,1:T(8,128)(2,1)S(1)}, u32[]{:S(2)}) copy-start(bf16[96,1,8,128]{3,2,0,1:T(8,128)(2,1)S(1)} %copy.216) | copy-start | bytes 589828
  145.9 6.5 %copy-start.90 = (pred[8,3]{1,0:T(8,128)(4,1)S(1)}, pred[8,3]{1,0:T(8,128)(4,1)}, u32[]{:S(2)}) copy-start(pred[8,3]{1,0:T(8,128)(4,1)} %copy.200) | copy-start | bytes 76
  146.8 7.0 %copy-start.12 = (bf16[96,1,8,128]{3,2,0,1:T(8,128)(2,1)}, bf16[96,1,8,128]{3,2,0,1:T(8,128)(2,1)S(1)}, u32[]{:S(2)}) copy-start(bf16[96,1,8,128]{3,2,0,1:T(8,128)(2,1)S(1)} %copy.218) | copy-start | bytes 589828
  148.6 5.2 %copy-start.14 = (bf16[96,1,8,128]{3,2,0,1:T(8,128)(2,1)}, bf16[96,1,8,128]{3,2,0,1:T(8,128)(2,1)S(1)}, u32[]{:S(2)}) copy-start(bf16[96,1,8,128]{3,2,0,1:T(8,128)(2,1)S(1)} %copy.220) | copy-start | bytes 589828
  149.4 5.6 %copy-start.5 = (bf16[1,1,512,1024]{3,2,1,0:T(8,128)(2,1)S(1)}, bf16[1,1,512,1024]{3,2,1,0:T(8,128)(2,1)}, u32[]{:S(2)}) copy-start(bf16[1,1,512,1024]{3,2,1,0:T(8,128)(2,1)} %get-tuple-element.13) | copy-start | bytes 3145732
  149.4 5.6 %copy-start.95 = (pred[8,16]{1,0:T(8,128)(4,1)S(1)}, pred[8,16]{1,0:T(8,128)(4,1)}, u32[]{:S(2)}) copy-start(pred[8,16]{1,0:T(8,128)(4,1)} %get-tuple-element.182) | copy-start | bytes 388
  149.4 5.6 %copy-start.99 = (pred[3,16]{1,0:T(4,128)(4,1)S(1)}, pred[3,16]{1,0:T(4,128)(4,1)}, u32[]{:S(2)}) copy-start(pred[3,16]{1,0:T(4,128)(4,1)} %iota_compare_fusion.11) | copy-start | bytes 148
  153.7 46.8 %collective-permute-start = (bf16[8,3,32,1024]{3,2,1,0:T(8,128)(2,1)}, bf16[8,3,32,1024]{3,2,1,0:T(8,128)(2,1)}, u32[]{:S(2)}, u32[]{:S(2)}) collective-permute-start(bf16[8,3,32,1024]{3,2,1,0:T(8,128)(2,1)} %broadcast_select_fusion.1), channel_id=1, source_target_pairs={{0,64},{1,65},{2,66},{3,67},{4,68},{5,69},{6,70},{7,71},{8,72},{9,... | collective-permute-start | bytes 4718600 | tf_op jit(solution)/shard_map/ppermute | solution.py:15
  157.9 4.3 %copy-start.81 = (pred[8,3,16]{2,0,1:T(8,128)(4,1)S(1)}, pred[8,3,16]{2,0,1:T(8,128)(4,1)}, u32[]{:S(2)}) copy-start(pred[8,3,16]{2,0,1:T(8,128)(4,1)} %copy-done.80) | copy-start | bytes 1156
  158.0 4.3 %copy-start.88 = (pred[8,1,16]{2,0,1:T(8,128)(4,1)S(1)}, pred[8,1,16]{2,0,1:T(8,128)(4,1)}, u32[]{:S(2)}) copy-start(pred[8,1,16]{2,0,1:T(8,128)(4,1)} %copy-done.87) | copy-start | bytes 388
  158.0 5.1 %copy-start.98 = (s32[16]{0:T(128)S(1)}, s32[16]{0:T(128)}, u32[]{:S(2)}) copy-start(s32[16]{0:T(128)} %get-tuple-element.179) | copy-start | bytes 196
  158.0 5.1 %copy-start.4 = (bf16[1,1,512,1024]{3,2,1,0:T(8,128)(2,1)S(1)}, bf16[1,1,512,1024]{3,2,1,0:T(8,128)(2,1)}, u32[]{:S(2)}) copy-start(bf16[1,1,512,1024]{3,2,1,0:T(8,128)(2,1)} %get-tuple-element.11) | copy-start | bytes 3145732
  158.0 5.1 %copy-start.94 = (pred[8,16]{1,0:T(8,128)(4,1)S(1)}, pred[8,16]{1,0:T(8,128)(4,1)}, u32[]{:S(2)}) copy-start(pred[8,16]{1,0:T(8,128)(4,1)} %get-tuple-element.181) | copy-start | bytes 388
  158.0 21.0 %all-to-all-start.1 = ((bf16[8,3,32,1024]{3,2,1,0:T(8,128)(2,1)}), bf16[8,3,32,1024]{3,2,1,0:T(8,128)(2,1)S(1)}, u32[]{:S(2)}, u32[]{:S(2)}) async-start(bf16[8,3,32,1024]{3,2,1,0:T(8,128)(2,1)} %copy.225), calls=%async_computation.1 | async-start | bytes 3145728 | tf_op jit(solution)/shard_map/all_to_all | solution.py:81
  161.7 141.2 %all-gather.22.cloned.1.call-start = ((), (), s32[]{:S(2)}) async-start(), calls=%async_computation.7 | async-start | bytes 1179648 | tf_op jit(solution)/shard_map/all_gather | solution.py:84
  179.0 71.6 %all-to-all-start.2 = ((bf16[8,3,32,1024]{3,2,1,0:T(8,128)(2,1)}), bf16[8,3,32,1024]{3,2,1,0:T(8,128)(2,1)}, u32[]{:S(2)}, u32[]{:S(2)}) async-start(bf16[8,3,32,1024]{3,2,1,0:T(8,128)(2,1)} %copy.255), calls=%async_computation.2 | async-start | bytes 3145728 | tf_op jit(solution)/shard_map/all_to_all | solution.py:81
  238.1 6.2 %copy-start.31 = (bf16[96,1,8,128]{3,2,0,1:T(8,128)(2,1)S(1)}, bf16[96,1,8,128]{3,2,0,1:T(8,128)(2,1)}, u32[]{:S(2)}) copy-start(bf16[96,1,8,128]{3,2,0,1:T(8,128)(2,1)} %copy-done.30) | copy-start | bytes 589828
  238.1 57.5 %collective-permute-start.1 = (bf16[8,3,32,1024]{3,2,1,0:T(8,128)(2,1)}, bf16[8,3,32,1024]{3,2,1,0:T(8,128)(2,1)}, u32[]{:S(2)}, u32[]{:S(2)}) collective-permute-start(bf16[8,3,32,1024]{3,2,1,0:T(8,128)(2,1)} %broadcast_select_fusion), channel_id=1, source_target_pairs={{0,64},{1,65},{2,66},{3,67},{4,68},{5,69},{6,70},{7,71},{8,72},{9,... | collective-permute-start | bytes 4718600 | tf_op jit(solution)/shard_map/ppermute | solution.py:15
  240.2 4.2 %copy-start.29 = (bf16[96,1,8,128]{3,2,0,1:T(8,128)(2,1)S(1)}, bf16[96,1,8,128]{3,2,0,1:T(8,128)(2,1)}, u32[]{:S(2)}) copy-start(bf16[96,1,8,128]{3,2,0,1:T(8,128)(2,1)} %copy-done.28) | copy-start | bytes 589828
  240.3 4.2 %copy-start.27 = (bf16[96,1,8,128]{3,2,0,1:T(8,128)(2,1)S(1)}, bf16[96,1,8,128]{3,2,0,1:T(8,128)(2,1)}, u32[]{:S(2)}) copy-start(bf16[96,1,8,128]{3,2,0,1:T(8,128)(2,1)} %copy-done.26) | copy-start | bytes 589828
  (83 other events, 164.5 us)
Sparse Core Ops, SparseCore 0:
  9.0 51.1 all-gather.15
  61.8 38.1 all-gather.13
  101.7 38.0 all-gather.19
  141.3 48.4 all-gather.17
  191.3 39.7 all-gather.23
  232.5 43.8 all-gather.21
where the time goes:
time: 342 us; the launch traced here: 337 us
  waiting for transfers between devices  72.9 us (21%)
  local copies, waits for them, and re-layouts  70.8 us (21%)
  blocking collectives  64.4 us (19%)
  matrix products  52.2 us (15%)
  other arithmetic  40.9 us (12%)
  starting transfers between devices  19.3 us (6%)
  between operations  16.2 us (5%)
    ppermute x2, waiting for transfers between devices, shifted(): return lax.ppermute(block, axis, route)  60.7 us
    all_gather x1, blocking collectives, local(): lax.all_gather(owners, 'ctx', axis=1, tiled=True)  36.3 us
    dot_general x24, matrix products, attend_rows(): jnp.einsum('tkgj,jkd->tkgd', weights, value_heads, preferred_element_type...  30.3 us
    all_gather x1, blocking collectives, local(): lax.all_gather(doc_start, 'ctx', axis=1, tiled=True)  28.1 us
    unnamed x269, local copies, waits for them, and re-layouts  23.5 us
    dot_general x24, matrix products, attend_rows(): jnp.einsum('tkgd,jkd->tkgj', heads_for_query, heads_for_key, preferred_el...  19.3 us
    reduce_sum x24, other arithmetic, attend_rows(): denom_sum = jnp.sum(exp_terms, axis=-1)  18 us
    all_to_all x3, starting transfers between devices, local(): lax.all_to_all(outgoing, 'ctx', split_axis=0, concat_axis=0, tiled=True)  16.4 us
  transfers between devices with their start and end apart: 11, of which 3 were waited for; matrix products, arithmetic and copies ran while one was open for 39% of the time, Pallas kernels for 0%

commit v1 on v0

--- a/solution.py
+++ b/solution.py
@@ -83,7 +83,9 @@
             lax.all_gather(key_rows, "ctx", axis=0, tiled=True),
             lax.all_gather(value_rows, "ctx", axis=0, tiled=True),
             lax.all_gather(owners, "ctx", axis=1, tiled=True),
-            lax.all_gather(doc_start, "ctx", axis=1, tiled=True),
+            jnp.concatenate(
+                lax.all_to_all(jnp.stack([doc_start] * lax.axis_size("ctx")), "ctx", 0, 0), axis=1
+            ),
         )
         section_in = (arrived.astype(jnp.float32) + carried.astype(jnp.float32)).astype(
             jnp.bfloat16

time: 342 us -> 320 us (0.936)
  blocking collectives: 64.4 us -> 17.8 us
  waiting for transfers between devices: 72.9 us -> 90.2 us
  starting transfers between devices: 19.3 us -> 25.6 us
    all_gather x1 -> x0, blocking collectives: 28.1 us -> none  [local(): lax.all_gather(doc_start, 'ctx', axis=1, tiled=True)]
    all_gather x3, waiting for transfers between devices: 0.01 us -> 19.1 us  [local(): lax.all_gather(value_rows, 'ctx', axis=0, tiled=True)]
    all_gather x1, blocking collectives: 36.3 us -> 17.8 us  [local(): lax.all_gather(owners, 'ctx', axis=1, tiled=True)]
    all_to_all x0 -> x1, starting transfers between devices: none -> 6.77 us  [local(): lax.all_to_all(jnp.stack([doc_start] * lax.axis_size('ctx')), 'ctx', 0, 0)]
    unnamed x269 -> x267, local copies, waits for them, and re-layouts: 23.5 us -> 23.5 us
  transfers between devices with their start and end apart: 11 -> 12, of which waited for: 3 -> 5; matrix products, arithmetic and copies ran while one was open for 39% -> 42% of each run, Pallas kernels for 0% -> 0%
where the time goes in v1:
time: 320 us; the launch traced here: 314 us
  waiting for transfers between devices  90.2 us (28%)
  local copies, waits for them, and re-layouts  71.4 us (22%)
  matrix products  52.2 us (16%)
  other arithmetic  40.9 us (13%)
  starting transfers between devices  25.6 us (8%)
  blocking collectives  17.8 us (6%)
  between operations  16.2 us (5%)
    ppermute x2, waiting for transfers between devices, shifted(): return lax.ppermute(block, axis, route)  59.3 us
    dot_general x24, matrix products, attend_rows(): jnp.einsum('tkgj,jkd->tkgd', weights, value_heads, preferred_element_type...  30.2 us
    unnamed x267, local copies, waits for them, and re-layouts  23.5 us
    dot_general x24, matrix products, attend_rows(): jnp.einsum('tkgd,jkd->tkgj', heads_for_query, heads_for_key, preferred_el...  19.3 us
    all_gather x3, waiting for transfers between devices, local(): lax.all_gather(value_rows, 'ctx', axis=0, tiled=True)  19.1 us
    reduce_sum x24, other arithmetic, attend_rows(): denom_sum = jnp.sum(exp_terms, axis=-1)  18 us
    all_gather x1, blocking collectives, local(): lax.all_gather(owners, 'ctx', axis=1, tiled=True)  17.8 us
    all_to_all x3, starting transfers between devices, local(): lax.all_to_all(outgoing, 'ctx', split_axis=0, concat_axis=0, tiled=True)  16 us
  transfers between devices with their start and end apart: 12, of which 5 were waited for; matrix products, arithmetic and copies ran while one was open for 42% of the time, Pallas kernels for 0%

profile of v1, /device:TPU:6, one launch (start us, length us, event | category | flops | bytes accessed | tf_op | source)
XLA Modules:
  0.0 314.2 jit_solution(14526371864968663006)
XLA Ops:
  6.5 1.9 constant_dynamic-slice_fusion.16
  8.6 1.8 constant_dynamic-slice_fusion.4
  13.0 6.8 %all-to-all-start = ((s32[8,2,512]{2,1,0:T(2,128)}), s32[8,2,512]{2,1,0:T(2,128)S(1)}, u32[]{:S(2)}, u32[]{:S(2)}) async-start(s32[8,2,512]{2,1,0:T(2,128)} %stack.95), calls=%async_computation | async-start | bytes 65536 | tf_op jit(solution)/shard_map/all_to_all | solution.py:87
  20.4 17.8 %all-gather.6 = s32[8,16,2]{1,2,0:T(2,128)S(1)} all-gather(s32[1,16,2]{1,2,0:T(2,128)S(1)} %bitcast.1574), channel_id=1, replica_groups=mesh['pipe'=2,'ctx'=8,'tp'=8] {'ctx'}, dimensions={0}, use_global_device_ids=true | all-gather | bytes 1152 | tf_op jit(solution)/shard_map/all_gather | solution.py:85
  42.5 1.7 constant_dynamic-slice_fusion
  45.9 2.0 copy.204
  50.3 5.0 %all-to-all-start.1 = ((bf16[8,3,32,1024]{3,2,1,0:T(8,128)(2,1)}), bf16[8,3,32,1024]{3,2,1,0:T(8,128)(2,1)S(1)}, u32[]{:S(2)}, u32[]{:S(2)}) async-start(bf16[8,3,32,1024]{3,2,1,0:T(8,128)(2,1)} %copy.204), calls=%async_computation.1 | async-start | bytes 3145728 | tf_op jit(solution)/shard_map/all_to_all | solution.py:81
  55.3 4.5 %gather_fusion.1 = s32[768]{0:T(1024)S(1)} fusion(s32[4096]{0:T(1024)S(1)} %bitcast.1518, s32[1024]{0:T(1024)S(1)} %pad_clamp_fusion.1), kind=kCustom, calls=%fused_computation.1 | custom fusion | bytes 9216 | tf_op jit(solution)/shard_map/gather | solution.py:111
  59.9 4.5 %gather_fusion = s32[768]{0:T(1024)S(1)} fusion(s32[4096]{0:T(1024)S(1)} %bitcast.1517, s32[1024]{0:T(1024)S(1)} %pad_clamp_fusion.2), kind=kCustom, calls=%fused_computation | custom fusion | bytes 9216 | tf_op jit(solution)/shard_map/gather | solution.py:111
  64.4 4.9 %gather_fusion.2 = s32[768]{0:T(1024)S(1)} fusion(s32[4096]{0:T(1024)S(1)} %bitcast.1516, s32[1024]{0:T(1024)S(1)} %pad_clamp_fusion), kind=kCustom, calls=%fused_computation.2 | custom fusion | bytes 9216 | tf_op jit(solution)/shard_map/gather | solution.py:111
  84.6 7.7 %all-gather.14.cloned.1.call-done = bf16[1,1,4096,128]{3,2,1,0:T(8,128)(2,1)} async-done(((bf16[1,1,512,128]{3,2,1,0:T(8,128)(2,1)}), bf16[1,1,4096,128]{3,2,1,0:T(8,128)(2,1)}) %all-gather.14.cloned.1.call-update) | async-done | bytes 1048592 | tf_op jit(solution)/shard_map/all_gather | solution.py:84
  92.3 1.8 fusion.429
  122.4 2.0 copy.225
  124.4 5.7 %all-to-all-start.2 = ((bf16[8,3,32,1024]{3,2,1,0:T(8,128)(2,1)}), bf16[8,3,32,1024]{3,2,1,0:T(8,128)(2,1)S(1)}, u32[]{:S(2)}, u32[]{:S(2)}) async-start(bf16[8,3,32,1024]{3,2,1,0:T(8,128)(2,1)} %copy.225), calls=%async_computation.2 | async-start | bytes 3145728 | tf_op jit(solution)/shard_map/all_to_all | solution.py:81
  132.5 2.0 copy.255
  137.7 9.4 %all-to-all-done.2 = bf16[8,3,32,1024]{3,2,1,0:T(8,128)(2,1)S(1)} async-done(((bf16[8,3,32,1024]{3,2,1,0:T(8,128)(2,1)}), bf16[8,3,32,1024]{3,2,1,0:T(8,128)(2,1)S(1)}, u32[]{:S(2)}, u32[]{:S(2)}) %all-to-all-start.2) | async-done | bytes 1572896 | tf_op jit(solution)/shard_map/all_to_all | solution.py:81
  147.0 5.3 %all-to-all-start.3 = ((bf16[8,3,32,1024]{3,2,1,0:T(8,128)(2,1)}), bf16[8,3,32,1024]{3,2,1,0:T(8,128)(2,1)}, u32[]{:S(2)}, u32[]{:S(2)}) async-start(bf16[8,3,32,1024]{3,2,1,0:T(8,128)(2,1)} %copy.255), calls=%async_computation.3 | async-start | bytes 3145728 | tf_op jit(solution)/shard_map/all_to_all | solution.py:81
  152.4 17.3 %collective-permute-done = bf16[8,3,32,1024]{3,2,1,0:T(8,128)(2,1)} collective-permute-done((bf16[8,3,32,1024]{3,2,1,0:T(8,128)(2,1)}, bf16[8,3,32,1024]{3,2,1,0:T(8,128)(2,1)}, u32[]{:S(2)}, u32[]{:S(2)}) %collective-permute-start) | collective-permute-done | bytes 1572896 | tf_op jit(solution)/shard_map/ppermute | solution.py:15
  169.6 2.1 add_convert_fusion.1
  176.4 11.4 %all-gather.18.cloned.1.call-done = bf16[1,1,4096,128]{3,2,1,0:T(8,128)(2,1)} async-done(((bf16[1,1,512,128]{3,2,1,0:T(8,128)(2,1)}), bf16[1,1,4096,128]{3,2,1,0:T(8,128)(2,1)}) %all-gather.18.cloned.1.call-update) | async-done | bytes 1048592 | tf_op jit(solution)/shard_map/all_gather | solution.py:84
  194.9 1.7 fusion.399
  202.2 1.7 fusion.393
  206.3 1.7 fusion.390
  214.3 1.7 fusion.384
  230.9 42.0 %collective-permute-done.1 = bf16[8,3,32,1024]{3,2,1,0:T(8,128)(2,1)} collective-permute-done((bf16[8,3,32,1024]{3,2,1,0:T(8,128)(2,1)}, bf16[8,3,32,1024]{3,2,1,0:T(8,128)(2,1)}, u32[]{:S(2)}, u32[]{:S(2)}) %collective-permute-start.1) | collective-permute-done | bytes 1572896 | tf_op jit(solution)/shard_map/ppermute | solution.py:15
  273.0 2.6 add_convert_fusion
  280.2 1.7 fusion.360
  291.6 1.7 fusion.372
  294.9 1.7 fusion.375
  298.2 1.7 fusion.378
  302.9 2.3 select_select_fusion.1
  305.2 1.9 maximum_bitcast_fusion
  (523 shorter events, 120.0 us)
Async XLA Ops:
  6.5 13.8 %copy-start.89 = (s32[2,16]{1,0:T(2,128)S(1)}, s32[2,16]{1,0:T(2,128)}, u32[]{:S(2)}) copy-start(s32[2,16]{1,0:T(2,128)} %param.9) | copy-start | bytes 388
  6.5 35.9 %copy-start.3 = (bf16[1,2,512,1024]{3,2,1,0:T(8,128)(2,1)S(1)}, bf16[1,2,512,1024]{3,2,1,0:T(8,128)(2,1)}, u32[]{:S(2)}) copy-start(bf16[1,2,512,1024]{3,2,1,0:T(8,128)(2,1)} %param.5) | copy-start | bytes 6291460
  6.5 75.3 %all-gather.16.cloned.1.call-start = ((), (), s32[]{:S(2)}) async-start(), calls=%async_computation.5 | async-start | bytes 1179648 | tf_op jit(solution)/shard_map/all_gather | solution.py:83
  8.5 83.8 %all-gather.14.cloned.1.call-start = ((), (), s32[]{:S(2)}) async-start(), calls=%async_computation.4 | async-start | bytes 1179648 | tf_op jit(solution)/shard_map/all_gather | solution.py:84
  10.4 162.5 %all-gather.20.cloned.1.call-start = ((), (), s32[]{:S(2)}) async-start(), calls=%async_computation.7 | async-start | bytes 1179648 | tf_op jit(solution)/shard_map/all_gather | solution.py:83
  11.1 176.6 %all-gather.18.cloned.1.call-start = ((), (), s32[]{:S(2)}) async-start(), calls=%async_computation.6 | async-start | bytes 1179648 | tf_op jit(solution)/shard_map/all_gather | solution.py:84
  13.0 37.3 %all-to-all-start = ((s32[8,2,512]{2,1,0:T(2,128)}), s32[8,2,512]{2,1,0:T(2,128)S(1)}, u32[]{:S(2)}, u32[]{:S(2)}) async-start(s32[8,2,512]{2,1,0:T(2,128)} %stack.95), calls=%async_computation | async-start | bytes 65536 | tf_op jit(solution)/shard_map/all_to_all | solution.py:87
  19.8 257.0 %all-gather.24.cloned.1.call-start = ((), (), s32[]{:S(2)}) async-start(), calls=%async_computation.9 | async-start | bytes 1179648 | tf_op jit(solution)/shard_map/all_gather | solution.py:83
  50.3 26.4 %all-to-all-start.1 = ((bf16[8,3,32,1024]{3,2,1,0:T(8,128)(2,1)}), bf16[8,3,32,1024]{3,2,1,0:T(8,128)(2,1)S(1)}, u32[]{:S(2)}, u32[]{:S(2)}) async-start(bf16[8,3,32,1024]{3,2,1,0:T(8,128)(2,1)} %copy.204), calls=%async_computation.1 | async-start | bytes 3145728 | tf_op jit(solution)/shard_map/all_to_all | solution.py:81
  83.3 9.0 %copy-start.84 = (f32[96,8]{0,1:T(8,128)}, f32[96,8]{0,1:T(8,128)S(1)}, u32[]{:S(2)}) copy-start(f32[96,8]{0,1:T(8,128)S(1)} %get-tuple-element.127) | copy-start | bytes 9220
  111.3 5.6 %copy-start.6 = (bf16[96,1,8,128]{3,2,0,1:T(8,128)(2,1)}, bf16[96,1,8,128]{3,2,0,1:T(8,128)(2,1)S(1)}, u32[]{:S(2)}) copy-start(bf16[96,1,8,128]{3,2,0,1:T(8,128)(2,1)S(1)} %copy.212) | copy-start | bytes 589828
  111.5 7.3 %copy-start.8 = (bf16[96,1,8,128]{3,2,0,1:T(8,128)(2,1)}, bf16[96,1,8,128]{3,2,0,1:T(8,128)(2,1)S(1)}, u32[]{:S(2)}) copy-start(bf16[96,1,8,128]{3,2,0,1:T(8,128)(2,1)S(1)} %copy.214) | copy-start | bytes 589828
  112.4 7.8 %copy-start.10 = (bf16[96,1,8,128]{3,2,0,1:T(8,128)(2,1)}, bf16[96,1,8,128]{3,2,0,1:T(8,128)(2,1)S(1)}, u32[]{:S(2)}) copy-start(bf16[96,1,8,128]{3,2,0,1:T(8,128)(2,1)S(1)} %copy.216) | copy-start | bytes 589828
  112.4 6.5 %copy-start.90 = (pred[8,3]{1,0:T(8,128)(4,1)S(1)}, pred[8,3]{1,0:T(8,128)(4,1)}, u32[]{:S(2)}) copy-start(pred[8,3]{1,0:T(8,128)(4,1)} %copy.200) | copy-start | bytes 76
  113.2 7.0 %copy-start.12 = (bf16[96,1,8,128]{3,2,0,1:T(8,128)(2,1)}, bf16[96,1,8,128]{3,2,0,1:T(8,128)(2,1)S(1)}, u32[]{:S(2)}) copy-start(bf16[96,1,8,128]{3,2,0,1:T(8,128)(2,1)S(1)} %copy.218) | copy-start | bytes 589828
  115.0 5.2 %copy-start.14 = (bf16[96,1,8,128]{3,2,0,1:T(8,128)(2,1)}, bf16[96,1,8,128]{3,2,0,1:T(8,128)(2,1)S(1)}, u32[]{:S(2)}) copy-start(bf16[96,1,8,128]{3,2,0,1:T(8,128)(2,1)S(1)} %copy.220) | copy-start | bytes 589828
  115.9 5.6 %copy-start.5 = (bf16[1,1,512,1024]{3,2,1,0:T(8,128)(2,1)S(1)}, bf16[1,1,512,1024]{3,2,1,0:T(8,128)(2,1)}, u32[]{:S(2)}) copy-start(bf16[1,1,512,1024]{3,2,1,0:T(8,128)(2,1)} %get-tuple-element.13) | copy-start | bytes 3145732
  115.9 5.6 %copy-start.95 = (pred[8,16]{1,0:T(8,128)(4,1)S(1)}, pred[8,16]{1,0:T(8,128)(4,1)}, u32[]{:S(2)}) copy-start(pred[8,16]{1,0:T(8,128)(4,1)} %get-tuple-element.182) | copy-start | bytes 388
  115.9 5.6 %copy-start.98 = (pred[3,16]{1,0:T(4,128)(4,1)S(1)}, pred[3,16]{1,0:T(4,128)(4,1)}, u32[]{:S(2)}) copy-start(pred[3,16]{1,0:T(4,128)(4,1)} %iota_compare_fusion.11) | copy-start | bytes 148
  120.2 49.4 %collective-permute-start = (bf16[8,3,32,1024]{3,2,1,0:T(8,128)(2,1)}, bf16[8,3,32,1024]{3,2,1,0:T(8,128)(2,1)}, u32[]{:S(2)}, u32[]{:S(2)}) collective-permute-start(bf16[8,3,32,1024]{3,2,1,0:T(8,128)(2,1)} %broadcast_select_fusion.1), channel_id=1, source_target_pairs={{0,64},{1,65},{2,66},{3,67},{4,68},{5,69},{6,70},{7,71},{8,72},{9,... | collective-permute-start | bytes 4718600 | tf_op jit(solution)/shard_map/ppermute | solution.py:15
  124.4 6.3 %copy-start.81 = (pred[8,3,16]{2,0,1:T(8,128)(4,1)S(1)}, pred[8,3,16]{2,0,1:T(8,128)(4,1)}, u32[]{:S(2)}) copy-start(pred[8,3,16]{2,0,1:T(8,128)(4,1)} %copy-done.80) | copy-start | bytes 1156
  124.4 6.3 %copy-start.88 = (pred[8,1,16]{2,0,1:T(8,128)(4,1)S(1)}, pred[8,1,16]{2,0,1:T(8,128)(4,1)}, u32[]{:S(2)}) copy-start(pred[8,1,16]{2,0,1:T(8,128)(4,1)} %copy-done.87) | copy-start | bytes 388
  124.4 7.1 %copy-start.97 = (s32[16]{0:T(128)S(1)}, s32[16]{0:T(128)}, u32[]{:S(2)}) copy-start(s32[16]{0:T(128)} %get-tuple-element.179) | copy-start | bytes 196
  124.4 7.1 %copy-start.4 = (bf16[1,1,512,1024]{3,2,1,0:T(8,128)(2,1)S(1)}, bf16[1,1,512,1024]{3,2,1,0:T(8,128)(2,1)}, u32[]{:S(2)}) copy-start(bf16[1,1,512,1024]{3,2,1,0:T(8,128)(2,1)} %get-tuple-element.11) | copy-start | bytes 3145732
  124.4 7.1 %copy-start.94 = (pred[8,16]{1,0:T(8,128)(4,1)S(1)}, pred[8,16]{1,0:T(8,128)(4,1)}, u32[]{:S(2)}) copy-start(pred[8,16]{1,0:T(8,128)(4,1)} %get-tuple-element.181) | copy-start | bytes 388
  124.4 22.6 %all-to-all-start.2 = ((bf16[8,3,32,1024]{3,2,1,0:T(8,128)(2,1)}), bf16[8,3,32,1024]{3,2,1,0:T(8,128)(2,1)S(1)}, u32[]{:S(2)}, u32[]{:S(2)}) async-start(bf16[8,3,32,1024]{3,2,1,0:T(8,128)(2,1)} %copy.225), calls=%async_computation.2 | async-start | bytes 3145728 | tf_op jit(solution)/shard_map/all_to_all | solution.py:81
  130.2 150.0 %all-gather.22.cloned.1.call-start = ((), (), s32[]{:S(2)}) async-start(), calls=%async_computation.8 | async-start | bytes 1179648 | tf_op jit(solution)/shard_map/all_gather | solution.py:84
  147.0 83.9 %all-to-all-start.3 = ((bf16[8,3,32,1024]{3,2,1,0:T(8,128)(2,1)}), bf16[8,3,32,1024]{3,2,1,0:T(8,128)(2,1)}, u32[]{:S(2)}, u32[]{:S(2)}) async-start(bf16[8,3,32,1024]{3,2,1,0:T(8,128)(2,1)} %copy.255), calls=%async_computation.3 | async-start | bytes 3145728 | tf_op jit(solution)/shard_map/all_to_all | solution.py:81
  176.4 14.2 %copy-start.1 = (bf16[1,1,4096,128]{3,2,1,0:T(8,128)(2,1)S(1)}, bf16[1,1,4096,128]{3,2,1,0:T(8,128)(2,1)}, u32[]{:S(2)}) copy-start(bf16[1,1,4096,128]{3,2,1,0:T(8,128)(2,1)} %all-gather.20.cloned.1.call-done) | copy-start | bytes 3145732
  176.4 14.2 %copy-start.76 = (pred[96,768]{1,0:T(8,128)(4,1)S(1)}, pred[96,768]{1,0:T(8,128)(4,1)}, u32[]{:S(2)}) copy-start(pred[96,768]{1,0:T(8,128)(4,1)} %get-tuple-element.104) | copy-start | bytes 221188
  218.4 6.2 %copy-start.31 = (bf16[96,1,8,128]{3,2,0,1:T(8,128)(2,1)S(1)}, bf16[96,1,8,128]{3,2,0,1:T(8,128)(2,1)}, u32[]{:S(2)}) copy-start(bf16[96,1,8,128]{3,2,0,1:T(8,128)(2,1)} %copy-done.30) | copy-start | bytes 589828
  218.4 54.5 %collective-permute-start.1 = (bf16[8,3,32,1024]{3,2,1,0:T(8,128)(2,1)}, bf16[8,3,32,1024]{3,2,1,0:T(8,128)(2,1)}, u32[]{:S(2)}, u32[]{:S(2)}) collective-permute-start(bf16[8,3,32,1024]{3,2,1,0:T(8,128)(2,1)} %broadcast_select_fusion), channel_id=1, source_target_pairs={{0,64},{1,65},{2,66},{3,67},{4,68},{5,69},{6,70},{7,71},{8,72},{9,... | collective-permute-start | bytes 4718600 | tf_op jit(solution)/shard_map/ppermute | solution.py:15
  (83 other events, 173.6 us)
Sparse Core Ops, SparseCore 0:
  9.0 41.1 all-gather.15
  51.9 40.3 all-gather.13
  93.9 41.7 all-gather.19
  137.2 50.5 all-gather.17
  189.2 38.4 all-gather.23
  229.2 40.2 all-gather.21
